TPU v7x, 32 devices: a whole 2x2x4 slice. The times are simulated.
32 devices in a mesh: row: 4 (over y, x), col: 8 (over z, core).
Axes of the slice: x: 2, y: 2, z: 4, core: 2. Of those that a mesh axis runs over, the one named last changes fastest.
Arguments:
- covariance: float32 [4096, 4096], P('row', 'col'), may hold values from -7 to 14, as said below
- wind_mask: int32 [2, 4096], replicated, may hold values 0 or 1
- wind_speed: float32 [2, 4096], replicated, may hold values from 0.02 to 0.3
- obs_cells: int32 [256, 128], replicated, may hold values from 0 to 4095
- obs_scale: float32 [256], replicated, may hold values from 0.05 to 0.2
- gain: bfloat16 [4096, 256], P('row'), may hold values from -0.375 to 0.375
Outputs:
- updated: float32 [4096, 4096], P('row', 'col')
Inputs may be any that keep to these rules, and one draw needn't show every extreme that they name: A covariance window.
All inputs are finite; a program needn't handle non-finite values.
Results may differ from a plain program's by a relative error of at most 0.0003.
Values sent between devices are 32-bit elements; how exact they have to be, the bound alone decides.
A program may use at most 64 MiB of HBM per device.

v0:
```python
import jax
import jax.numpy as jnp
from jax import lax
from jax.sharding import PartitionSpec as P

MAPX = 256


diffusion = 0.05


def extended_2(cells, sides, width):
    for axis, dim in sides:
        count = lax.axis_size(axis)
        ends = count - 1
        head = lax.slice_in_dim(cells, 0, width, axis=dim)
        tail = lax.slice_in_dim(cells, cells.shape[dim] - width, cells.shape[dim], axis=dim)
        cells = jnp.concatenate(
            [
                lax.ppermute(tail, axis, [(i, (i + 1) % count) for i in range(ends)]),
                cells,
                lax.ppermute(head, axis, [((i + 1) % count, i) for i in range(ends)]),
            ],
            axis=dim,
        )
    return cells


def coefficients(wind_mask, wind_speed):
    cell_total = wind_speed.shape[1]
    cells = jnp.arange(cell_total, dtype=jnp.int32)
    map_column = cells % MAPX
    map_row = cells // MAPX
    last_row = cell_total // MAPX - 1
    speed_x = wind_speed[0]
    speed_y = wind_speed[1]
    sign_x = wind_mask[0].astype(jnp.float32)
    sign_y = wind_mask[1].astype(jnp.float32)
    middle = 1.0 - speed_x - speed_y - 4.0 * diffusion
    western = jnp.where(map_column > 0, speed_x * sign_x + diffusion, 0.0)
    eastern = jnp.where(map_column < MAPX - 1, speed_x * (1.0 - sign_x) + diffusion, 0.0)
    northern = jnp.where(map_row > 0, speed_y * sign_y + diffusion, 0.0)
    southern = jnp.where(map_row < last_row, speed_y * (1.0 - sign_y) + diffusion, 0.0)
    return jnp.stack([middle, western, eastern, northern, southern])


def transport(extended, coef, along_dim):
    length = extended.shape[along_dim] - 2 * MAPX
    if along_dim == 0:
        weights = coef[:, :, None]
    else:
        weights = coef[:, None, :]

    def window_at(offset):
        return lax.slice_in_dim(extended, offset, offset + length, axis=along_dim)

    result = weights[0] * window_at(MAPX) + weights[1] * window_at(MAPX - 1)
    result = result + weights[2] * window_at(MAPX + 1)
    result = result + weights[3] * window_at(0) + weights[4] * window_at(2 * MAPX)
    return result


def local(covariance, wind_mask, wind_speed, obs_cells, obs_scale, gain):
    row_count, col_count = covariance.shape
    table = coefficients(wind_mask, wind_speed)
    row_start = lax.axis_index("row") * row_count
    col_start = lax.axis_index("col") * col_count
    row_coef = lax.dynamic_slice_in_dim(table, row_start, row_count, 1)

    def left_step(block):
        extended = extended_2(block, (("row", 0),), MAPX)
        return transport(extended, row_coef, 0)

    moved_field = left_step(left_step(covariance))
    padded_table = jnp.pad(table, ((0, 0), (2 * MAPX, 2 * MAPX)))
    extended = extended_2(moved_field, (("col", 1),), 2 * MAPX)
    wide_coef = lax.dynamic_slice_in_dim(padded_table, col_start + MAPX, col_count + 2 * MAPX, 1)
    first_pass = transport(extended, wide_coef, 1)
    inner_coef = lax.dynamic_slice_in_dim(padded_table, col_start + 2 * MAPX, col_count, 1)
    moved_field = transport(first_pass, inner_coef, 1)
    obs_count, foot_count = obs_cells.shape
    obs_block = 16
    local_cell = (obs_cells - row_start).reshape(obs_count // obs_block, obs_block, foot_count)
    row_ids = jnp.arange(row_count, dtype=jnp.int32)

    def count_block(cell_block):
        hits = (cell_block[:, :, None] == row_ids[None, None, :]).astype(jnp.float32)
        return jnp.sum(hits, axis=1)

    counts = lax.map(count_block, local_cell).reshape(obs_count, row_count)
    select = counts * obs_scale[:, None]
    part_sum = jnp.dot(
        select, moved_field, precision=lax.Precision.HIGHEST, preferred_element_type=jnp.float32
    )
    gain_panel = gain.astype(jnp.float32)
    observed = lax.psum(part_sum, "row")
    update = jnp.dot(
        gain_panel, observed, precision=lax.Precision.HIGHEST, preferred_element_type=jnp.float32
    )
    return moved_field - update


def solution(mesh):
    placed = (P("row", "col"), P(), P(), P(), P(), P("row", None))
    return jax.shard_map(
        local, mesh=mesh, in_specs=placed, out_specs=P("row", "col"), check_vma=False
    )
```

profile of v0, /device:TPU:8, one launch (start us, length us, event | category | flops | bytes accessed | tf_op | source)
XLA Modules:
  0.0 183.0 jit_solution(6771783297574050446)
XLA Ops:
  6.5 2.0 %copy.13 = f32[1024,512]{0,1:T(8,128)S(1)} copy(f32[1024,512]{1,0:T(8,128)} %param.8) | data formatting | bytes 4194304 | tf_op args[0]
  9.6 3.4 %collective-permute-start = (f32[256,512]{0,1:T(8,128)}, f32[256,512]{0,1:T(8,128)S(1)}, u32[]{:S(2)}, u32[]{:S(2)}) collective-permute-start(f32[256,512]{0,1:T(8,128)} %get-tuple-element.44), channel_id=1, source_target_pairs={{0,8},{8,16},{16,24},{1,9},{9,17},{17,25},{2,10},{10,18},{18,26},{... | collective-permute-start | bytes 1572872 | tf_op jit(solution)/shard_map/ppermute | solution.py:20
  14.8 9.7 %collective-permute-done = f32[256,512]{0,1:T(8,128)S(1)} collective-permute-done((f32[256,512]{0,1:T(8,128)}, f32[256,512]{0,1:T(8,128)S(1)}, u32[]{:S(2)}, u32[]{:S(2)}) %collective-permute-start) | collective-permute-done | bytes 524320 | tf_op jit(solution)/shard_map/ppermute | solution.py:20
  24.5 13.2 %collective-permute-done.1 = f32[256,512]{0,1:T(8,128)} collective-permute-done((f32[256,512]{0,1:T(8,128)}, f32[256,512]{0,1:T(8,128)}, u32[]{:S(2)}, u32[]{:S(2)}) %collective-permute-start.1) | collective-permute-done | bytes 524320 | tf_op jit(solution)/shard_map/ppermute | solution.py:22
  37.7 2.8 %fusion.18 = f32[1024,512]{0,1:T(8,128)S(1)} fusion(f32[1024,512]{0,1:T(8,128)S(1)} %copy.13, f32[256,512]{0,1:T(8,128)} %collective-permute-done.1, f32[256,512]{0,1:T(8,128)S(1)} %collective-permute-done, f32[1024]{0:T(1024)S(1)} %bitcast.41, f32[1024]{0:T(1024)S(1)} %bitcast.33, f32[1024]{0:T(1024)S(1)} %bitcast.35, f32[1024]{0:T(1024)S(1)} %bitcast.37, ...), kind=kLoop, calls=%fused_computation.35 | loop fusion | flops 6815744 | bytes 5263360 | tf_op jit(solution)/shard_map/add | solution.py:59
  41.9 3.4 %collective-permute-start.2 = (f32[256,512]{0,1:T(8,128)S(1)}, f32[256,512]{0,1:T(8,128)S(1)}, u32[]{:S(2)}, u32[]{:S(2)}) collective-permute-start(f32[256,512]{0,1:T(8,128)S(1)} %get-tuple-element.42), channel_id=1, source_target_pairs={{0,8},{8,16},{16,24},{1,9},{9,17},{17,25},{2,10},{10,18},{18,26},{... | collective-permute-start | bytes 1572872 | tf_op jit(solution)/shard_map/ppermute | solution.py:20
  46.7 8.9 %collective-permute-done.2 = f32[256,512]{0,1:T(8,128)S(1)} collective-permute-done((f32[256,512]{0,1:T(8,128)S(1)}, f32[256,512]{0,1:T(8,128)S(1)}, u32[]{:S(2)}, u32[]{:S(2)}) %collective-permute-start.2) | collective-permute-done | bytes 524320 | tf_op jit(solution)/shard_map/ppermute | solution.py:20
  55.6 12.1 %collective-permute-done.3 = f32[256,512]{0,1:T(8,128)} collective-permute-done((f32[256,512]{0,1:T(8,128)S(1)}, f32[256,512]{0,1:T(8,128)}, u32[]{:S(2)}, u32[]{:S(2)}) %collective-permute-start.3) | collective-permute-done | bytes 524320 | tf_op jit(solution)/shard_map/ppermute | solution.py:22
  67.7 5.2 %fusion.10 = f32[1024,512]{0,1:T(8,128)S(1)} fusion(f32[1024,512]{0,1:T(8,128)} %copy-done.1, f32[256,512]{0,1:T(8,128)} %collective-permute-done.3, f32[256,512]{0,1:T(8,128)S(1)} %collective-permute-done.2, f32[1024]{0:T(1024)S(1)} %bitcast.42, f32[1024]{0:T(1024)S(1)} %bitcast.34, f32[1024]{0:T(1024)S(1)} %bitcast.36, f32[1024]{0:T(1024)S(1)} %bitcast.38, ...), kind=kLoop, calls=%fused_computation.27 | loop fusion | flops 6815744 | bytes 5263360 | tf_op jit(solution)/shard_map/add | solution.py:59
  72.9 1.9 %collective-permute-start.4 = (f32[1024,512]{0,1:T(8,128)S(1)}, f32[1024,512]{0,1:T(8,128)}, u32[]{:S(2)}, u32[]{:S(2)}) collective-permute-start(f32[1024,512]{0,1:T(8,128)S(1)} %fusion.10), channel_id=1, source_target_pairs={{0,1},{1,2},{2,3},{3,4},{4,5},{5,6},{6,7},{8,9},{9,10},{10,11},{11... | collective-permute-start | bytes 6291464 | tf_op jit(solution)/shard_map/ppermute | solution.py:20
  74.8 3.6 %collective-permute-start.5 = (f32[1024,512]{0,1:T(8,128)S(1)}, f32[1024,512]{0,1:T(8,128)}, u32[]{:S(2)}, u32[]{:S(2)}) collective-permute-start(f32[1024,512]{0,1:T(8,128)S(1)} %fusion.10), channel_id=1, source_target_pairs={{1,0},{2,1},{3,2},{4,3},{5,4},{6,5},{7,6},{9,8},{10,9},{11,10},{12... | collective-permute-start | bytes 6291464 | tf_op jit(solution)/shard_map/ppermute | solution.py:22
  78.5 32.8 %while.11 = (s32[]{:T(128)}, f32[16,16,1024]{2,1,0:T(8,128)}, s32[16,16,128]{2,1,0:T(8,128)S(1)}, s32[]{:T(128)}) while((s32[]{:T(128)}, f32[16,16,1024]{2,1,0:T(8,128)}, s32[16,16,128]{2,1,0:T(8,128)S(1)}, s32[]{:T(128)}) %tuple.45), condition=%wide.region_2.3_spmd.clone, body=%wide.region_0.2_spmd.clone.sunk | while | flops 6275074 | bytes 221753 | solution.py:90
  78.5 1.4 convert_reduce_fusion.2
  80.6 1.4 convert_reduce_fusion.2
  82.6 1.4 convert_reduce_fusion.2
  84.7 1.4 convert_reduce_fusion.2
  86.7 1.4 convert_reduce_fusion.2
  88.8 1.4 convert_reduce_fusion.2
  90.8 1.4 convert_reduce_fusion.2
  92.9 1.4 convert_reduce_fusion.2
  94.9 1.4 convert_reduce_fusion.2
  97.0 1.4 convert_reduce_fusion.2
  99.0 1.4 convert_reduce_fusion.2
  103.1 1.4 convert_reduce_fusion.2
  105.2 1.4 convert_reduce_fusion.2
  107.2 1.4 convert_reduce_fusion.2
  112.8 2.8 %pad_maximum_fusion = f32[1024,1536]{0,1:T(8,128)S(1)} fusion(f32[1024,512]{0,1:T(8,128)} %collective-permute-done.5, f32[1024,512]{0,1:T(8,128)S(1)} %fusion.10, f32[1024,512]{0,1:T(8,128)} %collective-permute-done.4), kind=kLoop, calls=%fused_computation.5 | loop fusion | flops 3145728 | bytes 12582912 | tf_op jit(solution)/shard_map/concatenate | solution.py:18
  115.6 4.7 %fusion.4 = f32[1024,1024]{0,1:T(8,128)S(1)} fusion(f32[1024,1536]{0,1:T(8,128)S(1)} %pad_maximum_fusion, f32[1024,512]{0,1:T(8,128)S(1)} %fusion.10, f32[1024,512]{0,1:T(8,128)} %collective-permute-done.4, f32[1024,512]{0,1:T(8,128)} %collective-permute-done.5, f32[1024]{0:T(1024)S(1)} %bitcast.47, f32[1024]{0:T(1024)S(1)} %bitcast.44, ...), kind=kLoop, calls=%fused_computation.9 | loop fusion | flops 11534336 | bytes 23089152 | tf_op jit(solution)/shard_map/add | solution.py:59
  121.5 2.7 %fusion.32 = f32[256,512]{1,0:T(8,128)} fusion(f32[256,1024]{1,0:T(8,128)S(1)} %bitcast_multiply_fusion, f32[1024,512]{0,1:T(8,128)S(1)} %fusion.22), kind=kOutput, calls=%fused_computation.82 | convolution fusion | flops 1610612736 | bytes 3670016 | tf_op jit(solution)/shard_map/dot_general | solution.py:92
  124.3 44.8 %all-reduce.3.cloned.1.call-done = f32[256,512]{1,0:T(8,128)} async-done(((f32[256,512]{1,0:T(8,128)}), f32[256,512]{1,0:T(8,128)}) %all-reduce.3.cloned.1.call-update) | async-done | bytes 524304 | tf_op jit(solution)/shard_map/psum | solution.py:96
  169.1 4.2 %bitcast_subtract_fusion = f32[1024,512]{0,1:T(8,128)} fusion(f32[1024,512]{0,1:T(8,128)S(1)} %fusion.22, f32[256,512]{1,0:T(8,128)} %all-reduce.3.cloned.1.call-done, bf16[1024,256]{1,0:T(8,128)(2,1)S(1)} %copy-done), kind=kOutput, calls=%fused_computation.56 | convolution fusion | flops 1611137024 | bytes 5242880 | tf_op jit(solution)/shard_map/dot_general | solution.py:97
  173.3 2.9 %copy.18 = f32[1024,512]{1,0:T(8,128)} copy(f32[1024,512]{0,1:T(8,128)} %bitcast_subtract_fusion) | data formatting | bytes 4194304 | tf_op jit(solution)/shard_map/sub | solution.py:100
  (62 shorter events, 21.0 us)
Async XLA Ops:
  6.5 162.5 %copy-start = (bf16[1024,256]{1,0:T(8,128)(2,1)S(1)}, bf16[1024,256]{1,0:T(8,128)(2,1)}, u32[]{:S(2)}) copy-start(bf16[1024,256]{1,0:T(8,128)(2,1)} %param.13) | copy-start | bytes 1572868
  6.5 162.5 %all-reduce.3.cloned.1.call-start = ((), (), s32[]{:S(2)}) async-start(), calls=%async_computation | async-start | bytes 1048576 | tf_op jit(solution)/shard_map/psum | solution.py:96
  8.5 5.8 %copy-start.3 = (s32[2,4096]{1,0:T(2,128)S(1)}, s32[2,4096]{1,0:T(2,128)}, u32[]{:S(2)}) copy-start(s32[2,4096]{1,0:T(2,128)} %param.9) | copy-start | bytes 98308
  8.5 5.8 %copy-start.4 = (f32[2,4096]{1,0:T(2,128)S(1)}, f32[2,4096]{1,0:T(2,128)}, u32[]{:S(2)}) copy-start(f32[2,4096]{1,0:T(2,128)} %param.10) | copy-start | bytes 98308
  9.6 14.9 %collective-permute-start = (f32[256,512]{0,1:T(8,128)}, f32[256,512]{0,1:T(8,128)S(1)}, u32[]{:S(2)}, u32[]{:S(2)}) collective-permute-start(f32[256,512]{0,1:T(8,128)} %get-tuple-element.44), channel_id=1, source_target_pairs={{0,8},{8,16},{16,24},{1,9},{9,17},{17,25},{2,10},{10,18},{18,26},{... | collective-permute-start | bytes 1572872 | tf_op jit(solution)/shard_map/ppermute | solution.py:20
  13.0 24.6 %collective-permute-start.1 = (f32[256,512]{0,1:T(8,128)}, f32[256,512]{0,1:T(8,128)}, u32[]{:S(2)}, u32[]{:S(2)}) collective-permute-start(f32[256,512]{0,1:T(8,128)} %get-tuple-element.45), channel_id=1, source_target_pairs={{8,0},{16,8},{24,16},{9,1},{17,9},{25,17},{10,2},{18,10},{26,18},{... | collective-permute-start | bytes 1572872 | tf_op jit(solution)/shard_map/ppermute | solution.py:22
  40.5 1.3 copy-start.1
  41.8 4.8 %copy-start.2 = (s32[256,128]{1,0:T(8,128)S(1)}, s32[256,128]{1,0:T(8,128)}, u32[]{:S(2)}) copy-start(s32[256,128]{1,0:T(8,128)} %param.11) | copy-start | bytes 393220
  41.9 13.7 %collective-permute-start.2 = (f32[256,512]{0,1:T(8,128)S(1)}, f32[256,512]{0,1:T(8,128)S(1)}, u32[]{:S(2)}, u32[]{:S(2)}) collective-permute-start(f32[256,512]{0,1:T(8,128)S(1)} %get-tuple-element.42), channel_id=1, source_target_pairs={{0,8},{8,16},{16,24},{1,9},{9,17},{17,25},{2,10},{10,18},{18,26},{... | collective-permute-start | bytes 1572872 | tf_op jit(solution)/shard_map/ppermute | solution.py:20
  45.4 22.3 %collective-permute-start.3 = (f32[256,512]{0,1:T(8,128)S(1)}, f32[256,512]{0,1:T(8,128)}, u32[]{:S(2)}, u32[]{:S(2)}) collective-permute-start(f32[256,512]{0,1:T(8,128)S(1)} %get-tuple-element.43), channel_id=1, source_target_pairs={{8,0},{16,8},{24,16},{9,1},{17,9},{25,17},{10,2},{18,10},{26,18},{... | collective-permute-start | bytes 1572872 | tf_op jit(solution)/shard_map/ppermute | solution.py:22
  46.7 64.7 %copy-start.5 = (f32[256]{0:T(256)S(1)}, f32[256]{0:T(256)}, u32[]{:S(2)}) copy-start(f32[256]{0:T(256)} %param.12) | copy-start | bytes 3076
  72.9 39.9 %collective-permute-start.4 = (f32[1024,512]{0,1:T(8,128)S(1)}, f32[1024,512]{0,1:T(8,128)}, u32[]{:S(2)}, u32[]{:S(2)}) collective-permute-start(f32[1024,512]{0,1:T(8,128)S(1)} %fusion.10), channel_id=1, source_target_pairs={{0,1},{1,2},{2,3},{3,4},{4,5},{5,6},{6,7},{8,9},{9,10},{10,11},{11... | collective-permute-start | bytes 6291464 | tf_op jit(solution)/shard_map/ppermute | solution.py:20
  74.8 38.0 %collective-permute-start.5 = (f32[1024,512]{0,1:T(8,128)S(1)}, f32[1024,512]{0,1:T(8,128)}, u32[]{:S(2)}, u32[]{:S(2)}) collective-permute-start(f32[1024,512]{0,1:T(8,128)S(1)} %fusion.10), channel_id=1, source_target_pairs={{1,0},{2,1},{3,2},{4,3},{5,4},{6,5},{7,6},{9,8},{10,9},{11,10},{12... | collective-permute-start | bytes 6291464 | tf_op jit(solution)/shard_map/ppermute | solution.py:22
Sparse Core Ops, SparseCore 0:
  124.4 44.5 all-reduce.2
where the time goes:
time: 185 us; the launch traced here: 183 us
  waiting for transfers between devices  88.7 us (48%)
  other arithmetic  40.8 us (22%)
  local copies, waits for them, and re-layouts  17.8 us (10%)
  starting transfers between devices  15 us (8%)
  between operations  13.6 us (7%)
  matrix products  6.97 us (4%)
    psum x1, waiting for transfers between devices, local(): observed = lax.psum(part_sum, 'row')  44.8 us
    ppermute x3, waiting for transfers between devices, extended_2(): lax.ppermute(head, axis, [((i + 1) % count, i) for i in range(ends)])  25.3 us
    reduce_sum x16, other arithmetic, count_block(): return jnp.sum(hits, axis=1)  22.6 us
    ppermute x3, waiting for transfers between devices, extended_2(): lax.ppermute(tail, axis, [(i, (i + 1) % count) for i in range(ends)])  18.6 us
    add x4, other arithmetic, transport(): result + weights[3] * window_at(0) + weights[4] * window_at(2 * MAPX)  13.9 us
    dynamic_update_slice x16, local copies, waits for them, and re-layouts, local(): counts = lax.map(count_block, local_cell).reshape(obs_count, row_count)  10 us
    ppermute x3, starting transfers between devices, extended_2(): lax.ppermute(tail, axis, [(i, (i + 1) % count) for i in range(ends)])  8.76 us
    ppermute x3, starting transfers between devices, extended_2(): lax.ppermute(head, axis, [((i + 1) % count, i) for i in range(ends)])  6.23 us
  transfers between devices with their start and end apart: 7, of which 5 were waited for; matrix products, arithmetic and copies ran while one was open for 19% of the time, Pallas kernels for 0%

commit v1 on v0

v1 whole, which is shorter than its diff:
```python
import functools

import jax
import jax.numpy as jnp
from jax import lax
from jax.experimental import pallas as pl
from jax.experimental.pallas import tpu as pltpu
from jax.sharding import PartitionSpec as P

MAPX = 256
LANES = 128
CHUNK = 128
TILE = 16
diffusion = 0.05
MESH = pl.DeviceIdType.MESH


def split(x):
    high = x.astype(jnp.bfloat16)
    return high, (x - high.astype(jnp.float32)).astype(jnp.bfloat16)


def dot(a, b):
    return jnp.dot(a, b, preferred_element_type=jnp.float32)


def coef_block(mask_ref, speed_ref, g, map_rows):
    inside = jnp.logical_and(g >= 0, g < map_rows)
    start = pl.multiple_of(jnp.clip(g, 0, map_rows - 1) * MAPX, MAPX)
    where = pl.ds(start, MAPX)
    speed_x = speed_ref[0:1, where]
    speed_y = speed_ref[1:2, where]
    sign_x = mask_ref[0:1, where].astype(jnp.float32)
    sign_y = mask_ref[1:2, where].astype(jnp.float32)
    column = lax.broadcasted_iota(jnp.int32, (1, MAPX), 1)
    valid = jnp.where(inside, 1.0, 0.0)
    north = jnp.where(g > 0, valid, 0.0)
    south = jnp.where(g < map_rows - 1, valid, 0.0)
    return (
        (1.0 - speed_x - speed_y - 4.0 * diffusion) * valid,
        jnp.where(column > 0, speed_x * sign_x + diffusion, 0.0) * valid,
        jnp.where(column < MAPX - 1, speed_x * (1.0 - sign_x) + diffusion, 0.0) * valid,
        (speed_y * sign_y + diffusion) * north,
        (speed_y * (1.0 - sign_y) + diffusion) * south,
    )


def kernel(
    nr, nc, cov, mask_ref, speed_ref, cells_ref, scale_ref,
    moved_ref, obs_out,
    own, lh, rh, V, Y, ccol, crow, rc, sbuf, s2, tbuf, ah, al, part, rsbuf, obs,
    own_sem, zs, zr, hs, hr, rs_s, rs_r, ag_s, ag_r,
):
    rows, cols = cov.shape
    n_obs = cells_ref.shape[0]
    map_rows = speed_ref.shape[1] // MAPX
    H = 2 * MAPX
    rb, cb = rows // MAPX, cols // MAPX
    nchunk = rows // CHUNK
    half = nchunk // 2
    me_r, me_c = lax.axis_index("row"), lax.axis_index("col")
    has_up, has_down = me_r > 0, me_r < nr - 1
    has_left, has_right = me_c > 0, me_c < nc - 1
    up, down, left, right = me_r - 1, me_r + 1, me_c - 1, me_c + 1
    bits = []
    b = nr // 2
    while b:
        bits.append(b)
        b //= 2

    barrier = pltpu.get_barrier_semaphore()
    for flag, dev in ((has_up, (up, me_c)), (has_down, (down, me_c)), (has_left, (me_r, left)), (has_right, (me_r, right))):
        @pl.when(flag)
        def _(dev=dev):
            pl.semaphore_signal(barrier, inc=1, device_id=dev, device_id_type=MESH)
    partners = []
    for b in bits:
        upper = lax.rem(me_r // b, 2)
        partner = me_r + b - 2 * b * upper
        partners.append((upper, partner))
        if b > 1:
            pl.semaphore_signal(barrier, inc=1, device_id=(partner, me_c), device_id_type=MESH)
    own_copy = pltpu.make_async_copy(cov, own, own_sem)
    own_copy.start()
    peers = len(bits) - 1
    for flag in (has_up, has_down, has_left, has_right):
        peers = peers + flag.astype(jnp.int32)
    pl.semaphore_wait(barrier, peers)

    def chunk_base(d, lower):
        if lower:
            q = half // 2
            index = half + q + d - half * (d // q)
        else:
            index = d
        return pl.multiple_of(index * CHUNK, CHUNK)

    def zcopy(d, lower, side):
        base = chunk_base(d, lower)
        slot = d * 2 + lower
        dst = (rh, lh)[side]
        return pltpu.make_async_remote_copy(
            src_ref=cov.at[pl.ds(base, CHUNK), :], dst_ref=dst.at[pl.ds(base, CHUNK), :],
            send_sem=zs.at[side, slot], recv_sem=zr.at[side, slot],
            device_id=(me_r, (left, right)[side]), device_id_type=MESH)

    def hcopy(d, lower):
        base = chunk_base(d, lower)
        dst = base - H if lower else base + H + rows
        return pltpu.make_async_remote_copy(
            src_ref=V.at[:, pl.ds(H + base, CHUNK), :],
            dst_ref=V.at[:, pl.ds(pl.multiple_of(dst, CHUNK), CHUNK), :],
            send_sem=hs.at[lower, d], recv_sem=hr.at[lower, d],
            device_id=(down if lower else up, me_c), device_id_type=MESH)

    def zstart(d, _):
        for lower in (0, 1):
            @pl.when(has_left)
            def _():
                zcopy(d, lower, 0).start()

            @pl.when(has_right)
            def _():
                zcopy(d, lower, 1).start()
        return 0

    lax.fori_loop(0, half, zstart, 0)

    @pl.when(jnp.logical_not(has_left))
    def _():
        lh[...] = jnp.zeros_like(lh)

    @pl.when(jnp.logical_not(has_right))
    def _():
        rh[...] = jnp.zeros_like(rh)

    @pl.when(jnp.logical_not(has_up))
    def _():
        V[:, 0:H, :] = jnp.zeros((V.shape[0], H, LANES), jnp.float32)

    @pl.when(jnp.logical_not(has_down))
    def _():
        V[:, H + rows:, :] = jnp.zeros((V.shape[0], H, LANES), jnp.float32)

    for b in range(cb + 4):
        for k, v in enumerate(coef_block(mask_ref, speed_ref, me_c * cb + b - 2, map_rows)):
            ccol[b, k:k + 1, :] = v
    for b in range(rb + 4):
        for k, v in enumerate(coef_block(mask_ref, speed_ref, me_r * rb + b - 2, map_rows)):
            crow[b, k:k + 1, :] = v

    own_copy.wait()

    def col_step(v, first, count):
        out = []
        for i in range(count):
            c = [ccol[first + i, k:k + 1, :] for k in range(5)]
            x = v[i + 1]
            r = c[0] * x + c[1] * pltpu.roll(x, 1, 1)
            r = r + c[2] * pltpu.roll(x, MAPX - 1, 1)
            out.append(r + c[3] * v[i] + c[4] * v[i + 2])
        return out

    def col_chunk(base):
        def body(t, _):
            at = pl.ds(pl.multiple_of(base + t * TILE, TILE), TILE)
            v = [lh[at, cols - H + j * MAPX:cols - H + (j + 1) * MAPX] for j in range(2)]
            v += [own[at, j * MAPX:(j + 1) * MAPX] for j in range(cb)]
            v += [rh[at, j * MAPX:(j + 1) * MAPX] for j in range(2)]
            y = col_step(v, 1, cb + 2)
            z = col_step(y, 2, cb)
            put = pl.ds(pl.multiple_of(H + base + t * TILE, TILE), TILE)
            for j in range(cb):
                for l in range(2):
                    V[2 * j + l, put, :] = z[j][:, l * LANES:(l + 1) * LANES]
            return 0
        lax.fori_loop(0, CHUNK // TILE, body, 0)

    wide = rows + 2 * H
    nh = wide // LANES
    origin = me_r * rows - H
    lo_iota = lax.broadcasted_iota(jnp.int32, (LANES, LANES), 0)
    hi_iota = lax.broadcasted_iota(jnp.int32, (nh, LANES), 0)

    def count_group(g, _):
        base = pl.multiple_of(g * 8, 8)
        idx = cells_ref[pl.ds(base, 8), :] - origin
        hi = lax.shift_right_arithmetic(idx, 7)
        lo = jnp.bitwise_and(idx, LANES - 1)
        for i in range(8):
            one_hi = jnp.where(hi[i:i + 1, :] == hi_iota, 1.0, 0.0).astype(jnp.bfloat16)
            one_lo = jnp.where(lo[i:i + 1, :] == lo_iota, 1.0, 0.0).astype(jnp.bfloat16)
            counts = lax.dot_general(one_hi, one_lo, (((1,), (1,)), ((), ())), preferred_element_type=jnp.float32)
            sbuf[pl.ds(pl.multiple_of((base + i) * nh, 8), nh), :] = counts * scale_ref[base + i]
        return 0

    nrc = (rows + H) // LANES
    groups = n_obs // 8
    for d in range(half):
        for lower in (0, 1):
            @pl.when(has_left)
            def _():
                zcopy(d, lower, 0).wait_send()
                zcopy(d, lower, 1).wait_recv()

            @pl.when(has_right)
            def _():
                zcopy(d, lower, 1).wait_send()
                zcopy(d, lower, 0).wait_recv()
            col_chunk(chunk_base(d, lower))

            @pl.when(has_down if lower else has_up)
            def _():
                hcopy(d, lower).start()
        if d < half - 1:
            g0 = groups * d // (half - 1)
            g1 = groups * (d + 1) // (half - 1)
            lax.fori_loop(g0, g1, count_group, 0)
        if d == half - 2:
            for h in range(nh):
                s2[h // 2, :, (h % 2) * LANES:(h % 2 + 1) * LANES] = sbuf[pl.ds(h, n_obs, stride=nh), :]

            def adjoint(src, at, b, offset):
                def get(i):
                    return src[i - offset, at, :]
                c = [crow[b, k:k + 1, :] for k in range(3)]
                x = get(b)
                r = c[0] * x + pltpu.roll(c[1] * x, MAPX - 1, 1) + pltpu.roll(c[2] * x, 1, 1)
                return r + crow[b + 1, 3:4, :] * get(b + 1) + crow[b - 1, 4:5, :] * get(b - 1)

            def step_one(t, _):
                at = pl.ds(pl.multiple_of(t * TILE, TILE), TILE)
                for b in range(1, rb + 3):
                    tbuf[b - 1, at, :] = adjoint(s2, at, b, 0)
                return 0

            def step_two(t, _):
                at = pl.ds(pl.multiple_of(t * TILE, TILE), TILE)
                for b in range(2, rb + 2):
                    a_hi, a_lo = split(adjoint(tbuf, at, b, 1))
                    ah[b - 2, at, :] = a_hi
                    al[b - 2, at, :] = a_lo
                return 0

            lax.fori_loop(0, n_obs // TILE, step_one, 0)
            lax.fori_loop(0, n_obs // TILE, step_two, 0)
            for b in (0, rb - 1):
                observe_block(V, ah, al, part, b, b == 0, H, cols)
    for b in range(1, rb - 1):
        observe_block(V, ah, al, part, b, False, H, cols)

    def rs_copy(s):
        upper, partner = partners[s]
        size = n_obs >> (s + 1)
        src = offs[s] + (1 - upper) * size
        return pltpu.make_async_remote_copy(
            src_ref=part.at[pl.ds(pl.multiple_of(src, 8), size), :],
            dst_ref=rsbuf.at[pl.ds(n_obs - 2 * size, size), :],
            send_sem=rs_s.at[s], recv_sem=rs_r.at[s], device_id=(partner, me_c), device_id_type=MESH)

    offs = [jnp.int32(0)]
    for s in range(len(bits)):
        offs.append(offs[s] + partners[s][0] * (n_obs >> (s + 1)))

    def rs_finish(s):
        size = n_obs >> (s + 1)
        copy = rs_copy(s)
        copy.wait()
        at = pl.ds(pl.multiple_of(offs[s + 1], 8), size)
        part[at, :] = part[at, :] + rsbuf[n_obs - 2 * size:n_obs - size, :]

    def ag_copy(s):
        size = n_obs >> (s + 1)
        at = pl.ds(pl.multiple_of(offs[s + 1], 8), size)
        return pltpu.make_async_remote_copy(
            src_ref=obs.at[at, :], dst_ref=obs.at[at, :],
            send_sem=ag_s.at[s], recv_sem=ag_r.at[s], device_id=(partners[s][1], me_c), device_id_type=MESH)

    def row_coefs():
        for b in range(rb + 2):
            for k in range(5):
                for l in range(2):
                    line = crow[b + 1, k:k + 1, l * LANES:(l + 1) * LANES]
                    rc[k, (2 * b + l) * LANES:(2 * b + l + 1) * LANES, :] = jnp.transpose(
                        jnp.broadcast_to(line, (LANES, LANES)))

    def row_block(src, src_off, dst, b):
        def body(t, _):
            r0 = b * MAPX + t * TILE
            w = [rc[k, pl.ds(pl.multiple_of(MAPX + r0, 8), TILE), :] for k in range(5)]
            for l in range(V.shape[0]):
                def get(offset):
                    return src[l, pl.ds(src_off + r0 + offset, TILE), :]
                r = w[0] * get(0) + w[1] * get(-1)
                r = r + w[2] * get(1)
                r = r + w[3] * get(-MAPX) + w[4] * get(MAPX)
                dst(l, r0, r)
            return 0
        lax.fori_loop(0, MAPX // TILE, body, 0)

    def to_y(l, r0, r):
        Y[l, pl.ds(pl.multiple_of(MAPX + r0, 8), TILE), :] = r

    def to_out(l, r0, r):
        moved_ref[pl.ds(pl.multiple_of(r0, 8), TILE), l * LANES:(l + 1) * LANES] = r

    n_stage = len(bits)
    rs_copy(0).start()
    row_coefs()
    for b in range(1, rb - 1):
        row_block(V, H, to_y, b)
    for s in range(n_stage):
        rs_finish(s)
        if s + 1 < n_stage:
            rs_copy(s + 1).start()
    mine = pl.ds(pl.multiple_of(offs[n_stage], 8), n_obs >> n_stage)
    obs[mine, :] = part[mine, :]

    def halo_wait(d):
        @pl.when(has_up)
        def _():
            hcopy(d, 0).wait_send()
            hcopy(d, 1).wait_recv()

        @pl.when(has_down)
        def _():
            hcopy(d, 1).wait_send()
            hcopy(d, 0).wait_recv()

    for s in reversed(range(n_stage)):
        ag_copy(s).start()
        if s == n_stage - 1:
            for d in range(half // 2):
                halo_wait(d)
            row_block(V, H, to_y, 0)
            row_block(V, H, to_y, rb - 1)
            for b in range(1, rb - 1):
                row_block(Y, MAPX, to_out, b)
        ag_copy(s).wait()
    obs_out[...] = obs[...]
    for d in range(half // 2, half):
        halo_wait(d)
    row_block(V, H, to_y, -1)
    row_block(V, H, to_y, rb)
    row_block(Y, MAPX, to_out, 0)
    row_block(Y, MAPX, to_out, rb - 1)


def observe_block(V, ah, al, part, b, first, H, cols):
    a_hi, a_lo = ah[b], al[b]
    for j in range(cols // MAPX):
        rows = slice(H + b * MAPX, H + (b + 1) * MAPX)
        x = jnp.concatenate([V[2 * j, rows, :], V[2 * j + 1, rows, :]], axis=1)
        x_hi, x_lo = split(x)
        r = dot(a_hi, x_hi) + dot(a_hi, x_lo) + dot(a_lo, x_hi)
        at = slice(j * MAPX, (j + 1) * MAPX)
        if first:
            part[:, at] = r
        else:
            part[:, at] = part[:, at] + r


def update_kernel(moved_ref, gain_ref, obs_ref, out_ref):
    o_hi, o_lo = split(obs_ref[...])
    g = gain_ref[...]
    out_ref[...] = moved_ref[...] - (dot(g, o_hi) + dot(g, o_lo))


def local(nr, nc, covariance, wind_mask, wind_speed, obs_cells, obs_scale, gain):
    rows, cols = covariance.shape
    n_obs = obs_cells.shape[0]
    H = 2 * MAPX
    nl = cols // LANES
    rb, cb = rows // MAPX, cols // MAPX
    nchunk = rows // CHUNK
    stages = nr.bit_length() - 1
    f32, bf16 = jnp.float32, jnp.bfloat16
    vmem = pl.BlockSpec(memory_space=pltpu.VMEM)
    dma = pltpu.SemaphoreType.DMA
    moved, obs = pl.pallas_call(
        functools.partial(kernel, nr, nc),
        out_shape=(jax.ShapeDtypeStruct((rows, cols), f32), jax.ShapeDtypeStruct((n_obs, cols), f32)),
        in_specs=[pl.BlockSpec(memory_space=pl.ANY), vmem, vmem, vmem, pl.BlockSpec(memory_space=pltpu.SMEM)],
        out_specs=(vmem, vmem),
        scratch_shapes=[
            pltpu.VMEM((rows, cols), f32),
            pltpu.VMEM((rows, cols), f32),
            pltpu.VMEM((rows, cols), f32),
            pltpu.VMEM((nl, rows + 2 * H, LANES), f32),
            pltpu.VMEM((nl, rows + H, LANES), f32),
            pltpu.VMEM((cb + 4, 8, MAPX), f32),
            pltpu.VMEM((rb + 4, 8, MAPX), f32),
            pltpu.VMEM((5, rows + H, LANES), f32),
            pltpu.VMEM((n_obs * (rows + 2 * H) // LANES, LANES), f32),
            pltpu.VMEM((rb + 4, n_obs, MAPX), f32),
            pltpu.VMEM((rb + 2, n_obs, MAPX), f32),
            pltpu.VMEM((rb, n_obs, MAPX), bf16),
            pltpu.VMEM((rb, n_obs, MAPX), bf16),
            pltpu.VMEM((n_obs, cols), f32),
            pltpu.VMEM((n_obs, cols), f32),
            pltpu.VMEM((n_obs, cols), f32),
            dma(()),
            dma((2, nchunk)), dma((2, nchunk)),
            dma((2, nchunk // 2)), dma((2, nchunk // 2)),
            dma((stages,)), dma((stages,)), dma((stages,)), dma((stages,)),
        ],
        compiler_params=pltpu.CompilerParams(
            collective_id=0, has_side_effects=True, vmem_limit_bytes=48 * 1024 * 1024),
        cost_estimate=pl.CostEstimate(flops=2 * 10 ** 9, bytes_accessed=10 ** 7, transcendentals=0),
    )(covariance, wind_mask, wind_speed, obs_cells, obs_scale)
    block = MAPX
    return pl.pallas_call(
        update_kernel,
        grid=(rows // block,),
        out_shape=jax.ShapeDtypeStruct((rows, cols), f32),
        in_specs=[
            pl.BlockSpec((block, cols), lambda i: (i, 0)),
            pl.BlockSpec((block, n_obs), lambda i: (i, 0)),
            pl.BlockSpec((n_obs, cols), lambda i: (0, 0)),
        ],
        out_specs=pl.BlockSpec((block, cols), lambda i: (i, 0)),
        cost_estimate=pl.CostEstimate(flops=10 ** 9, bytes_accessed=5 * 10 ** 6, transcendentals=0),
        compiler_params=pltpu.CompilerParams(vmem_limit_bytes=24 * 1024 * 1024),
    )(moved, gain, obs)


def solution(mesh):
    placed = (P("row", "col"), P(), P(), P(), P(), P("row", None))
    return jax.shard_map(
        functools.partial(local, mesh.shape["row"], mesh.shape["col"]),
        mesh=mesh, in_specs=placed, out_specs=P("row", "col"), check_vma=False
    )
```

time: 185 us -> 79.8 us (0.43)
  waiting for transfers between devices: 88.7 us -> 0 us
  Pallas kernels: 0 us -> 74.7 us
  other arithmetic: 40.8 us -> 0 us
  starting transfers between devices: 15 us -> 0 us
  between operations: 13.6 us -> 0.02 us
  local copies, waits for them, and re-layouts: 17.8 us -> 4.75 us
  matrix products: 6.97 us -> 0 us
    pallas_call x0 -> x2, Pallas kernels: none -> 74.7 us  [the longest x1 72.1 us: local(): pl.pallas_call(functools.partial(kernel, nr, nc), out_shape=(jax.ShapeDty...]
    psum x1 -> x0, waiting for transfers between devices: 44.8 us -> none  [local(): observed = lax.psum(part_sum, 'row')]
    ppermute x6 -> x0, waiting for transfers between devices: 43.9 us -> none  [the longest x3 25.3 us: extended_2(): lax.ppermute(head, axis, [((i + 1) % count, i) for i in range(ends)])]
    reduce_sum x16 -> x0, other arithmetic: 22.6 us -> none  [count_block(): return jnp.sum(hits, axis=1)]
    ppermute x6 -> x0, starting transfers between devices: 15 us -> none  [the longest x3 8.76 us: extended_2(): lax.ppermute(tail, axis, [(i, (i + 1) % count) for i in range(ends)])]
    add x4 -> x0, other arithmetic: 13.9 us -> none  [transport(): result + weights[3] * window_at(0) + weights[4] * window_at(2 * MAPX)]
    dynamic_update_slice x16 -> x0, local copies, waits for them, and re-layouts: 10 us -> none  [local(): counts = lax.map(count_block, local_cell).reshape(obs_count, row_count)]
    dot_general x2 -> x0, matrix products: 6.97 us -> none  [the longest x1 4.23 us: local(): jnp.dot(gain_panel, observed, precision=lax.Precision.HIGHEST, preferred_...]
  transfers between devices with their start and end apart: 7 -> 0, of which waited for: 5 -> 0; matrix products, arithmetic and copies ran while one was open for 19% -> 0% of each run, Pallas kernels for 0% -> 0%
where the time goes in v1:
time: 79.8 us; the launch traced here: 79.5 us
  Pallas kernels  74.7 us (94%)
  local copies, waits for them, and re-layouts  4.75 us (6%)
    pallas_call x1, Pallas kernels, local(): pl.pallas_call(functools.partial(kernel, nr, nc), out_shape=(jax.ShapeDty...  72.1 us
    unnamed x12, local copies, waits for them, and re-layouts  4.75 us
    pallas_call x1, Pallas kernels, local(): pl.pallas_call(update_kernel, grid=(rows // block,), out_shape=jax.ShapeD...  2.6 us

profile of v1, /device:TPU:8, one launch (start us, length us, event | category | flops | bytes accessed | tf_op | source)
XLA Modules:
  0.0 79.5 jit_solution(3492625811589313260)
XLA Ops:
  0.0 0.0 copy-start
  0.0 0.0 copy-start.1
  0.0 1.6 %copy-done.1 = f32[1024,512]{1,0:T(8,128)S(1)} copy-done((f32[1024,512]{1,0:T(8,128)S(1)}, f32[1024,512]{1,0:T(8,128)}, u32[]{:S(2)}) %copy-start.1) | copy-done | bytes 2097176
  1.7 0.0 copy-start.2
  1.7 0.9 %copy-done.2 = s32[256,128]{1,0:T(8,128)S(1)} copy-done((s32[256,128]{1,0:T(8,128)S(1)}, s32[256,128]{1,0:T(8,128)}, u32[]{:S(2)}) %copy-start.2) | copy-done | bytes 131096
  2.6 0.0 copy-start.3
  2.6 0.8 copy-done.3
  3.3 0.0 copy-start.4
  3.3 0.8 copy-done.4
  4.1 0.0 copy-start.5
  4.1 0.7 copy-done.5
  4.8 72.1 %shard_map.64 = (f32[1024,512]{1,0:T(8,128)S(1)}, f32[256,512]{1,0:T(8,128)S(1)}) custom-call(f32[1024,512]{1,0:T(8,128)S(1)} %copy-done.1, s32[2,4096]{1,0:T(2,128)S(1)} %copy-done.3, f32[2,4096]{1,0:T(2,128)S(1)} %copy-done.4, s32[256,128]{1,0:T(8,128)S(1)} %copy-done.2, f32[256]{0:T(256)S(1)} %copy-done.5), custom_call_target="tpu_custom_call" | custom-call | flops 2000000000 | bytes 10000000 | tf_op jit(solution)/shard_map/pallas_call | solution.py:380
  76.9 0.0 copy-done
  76.9 2.6 %shard_map.65 = f32[1024,512]{1,0:T(8,128)} custom-call(f32[1024,512]{1,0:T(8,128)S(1)} %get-tuple-element.7.moved_ref, bf16[1024,256]{1,0:T(8,128)(2,1)S(1)} %copy-done, f32[256,512]{1,0:T(8,128)S(1)} %get-tuple-element.8.obs_ref), custom_call_target="tpu_custom_call" | custom-call | flops 1000000000 | bytes 5000000 | tf_op jit(solution)/shard_map/pallas_call | solution.py:412
Async XLA Ops:
  0.0 76.9 %copy-start = (bf16[1024,256]{1,0:T(8,128)(2,1)S(1)}, bf16[1024,256]{1,0:T(8,128)(2,1)}, u32[]{:S(2)}) copy-start(bf16[1024,256]{1,0:T(8,128)(2,1)} %gain_ref.1) | copy-start | bytes 1572868
  0.0 1.6 %copy-start.1 = (f32[1024,512]{1,0:T(8,128)S(1)}, f32[1024,512]{1,0:T(8,128)}, u32[]{:S(2)}) copy-start(f32[1024,512]{1,0:T(8,128)} %cov.1) | copy-start | bytes 6291460
  1.7 0.9 %copy-start.2 = (s32[256,128]{1,0:T(8,128)S(1)}, s32[256,128]{1,0:T(8,128)}, u32[]{:S(2)}) copy-start(s32[256,128]{1,0:T(8,128)} %cells_ref.1) | copy-start | bytes 393220
  2.6 0.8 copy-start.3
  3.3 0.8 copy-start.4
  4.1 0.7 copy-start.5

commit v2 on v1

--- a/solution.py
+++ b/solution.py
@@ -46,8 +46,10 @@
 
 
 def kernel(
-    nr, nc, cov, mask_ref, speed_ref, cells_ref, scale_ref,
-    moved_ref, obs_out,
+    nr, nc, cov, mask_hbm, speed_hbm, cells_hbm, scale_hbm,
+    moved_out, obs_out,
+    moved_ref, out_sem,
+    mask_ref, speed_ref, cells_ref, scale_ref, in_sem, relay_buf, rl_s, rl_r, fw_s,
     own, lh, rh, V, Y, ccol, crow, rc, sbuf, s2, tbuf, ah, al, part, rsbuf, obs,
     own_sem, zs, zr, hs, hr, rs_s, rs_r, ag_s, ag_r,
 ):
@@ -81,6 +83,13 @@
         if b > 1:
             pl.semaphore_signal(barrier, inc=1, device_id=(partner, me_c), device_id_type=MESH)
     own_copy = pltpu.make_async_copy(cov, own, own_sem)
+    small = [
+        pltpu.make_async_copy(src, dst, in_sem.at[i])
+        for i, (src, dst) in enumerate((
+            (mask_hbm, mask_ref), (speed_hbm, speed_ref), (cells_hbm, cells_ref), (scale_hbm, scale_ref)))
+    ]
+    for copy in small:
+        copy.start()
     own_copy.start()
     peers = len(bits) - 1
     for flag in (has_up, has_down, has_left, has_right):
@@ -113,6 +122,68 @@
             send_sem=hs.at[lower, d], recv_sem=hr.at[lower, d],
             device_id=(down if lower else up, me_c), device_id_type=MESH)
 
+    relay = nr == 4
+
+    def far(lower):
+        return me_r == (nr // 2 - 1 if lower else nr // 2)
+
+    def corner(lower):
+        return me_r == (nr - 1 if lower else 0)
+
+    def relayed(d):
+        return relay and d % 2 == 0
+
+    def rcopy(d, lower):
+        return pltpu.make_async_remote_copy(
+            src_ref=V.at[:, pl.ds(H + chunk_base(d, lower), CHUNK), :], dst_ref=relay_buf.at[d // 2],
+            send_sem=rl_s.at[d // 2], recv_sem=rl_r.at[d // 2],
+            device_id=(me_r + nr // 2 if lower else me_r - nr // 2, me_c), device_id_type=MESH)
+
+    def fcopy(d, lower):
+        base = chunk_base(d, lower)
+        dst = base - H if lower else base + H + rows
+        return pltpu.make_async_remote_copy(
+            src_ref=relay_buf.at[d // 2],
+            dst_ref=V.at[:, pl.ds(pl.multiple_of(dst, CHUNK), CHUNK), :],
+            send_sem=fw_s.at[d // 2], recv_sem=hr.at[lower, d],
+            device_id=(up if lower else down, me_c), device_id_type=MESH)
+
+    def forward(d):
+        if relayed(d):
+            for lower in (0, 1):
+                @pl.when(corner(lower))
+                def _():
+                    rcopy(d, lower).wait_recv()
+                    fcopy(d, lower).start()
+
+    def hstart(d, lower):
+        flag = has_down if lower else has_up
+        if relayed(d):
+            @pl.when(far(lower))
+            def _():
+                rcopy(d, lower).start()
+            flag = jnp.logical_and(flag, jnp.logical_not(far(lower)))
+
+        @pl.when(flag)
+        def _():
+            hcopy(d, lower).start()
+
+    def hsent(d, lower):
+        flag = has_down if lower else has_up
+        if relayed(d):
+            @pl.when(far(lower))
+            def _():
+                rcopy(d, lower).wait_send()
+
+            @pl.when(corner(lower))
+            def _():
+                fcopy(d, lower).wait_send()
+            flag = jnp.logical_and(flag, jnp.logical_not(far(lower)))
+
+        @pl.when(flag)
+        def _():
+            hcopy(d, lower).wait_send()
+
     def zstart(d, _):
         for lower in (0, 1):
             @pl.when(has_left)
@@ -142,6 +213,8 @@
     def _():
         V[:, H + rows:, :] = jnp.zeros((V.shape[0], H, LANES), jnp.float32)
 
+    for copy in small:
+        copy.wait()
     for b in range(cb + 4):
         for k, v in enumerate(coef_block(mask_ref, speed_ref, me_c * cb + b - 2, map_rows)):
             ccol[b, k:k + 1, :] = v
@@ -208,10 +281,9 @@
                 zcopy(d, lower, 1).wait_send()
                 zcopy(d, lower, 0).wait_recv()
             col_chunk(chunk_base(d, lower))
-
-            @pl.when(has_down if lower else has_up)
-            def _():
-                hcopy(d, lower).start()
+            hstart(d, lower)
+        if d > 0 and d < half - 1:
+            forward(d - 1)
         if d < half - 1:
             g0 = groups * d // (half - 1)
             g1 = groups * (d + 1) // (half - 1)
@@ -304,8 +376,13 @@
     def to_out(l, r0, r):
         moved_ref[pl.ds(pl.multiple_of(r0, 8), TILE), l * LANES:(l + 1) * LANES] = r
 
+    def put(b):
+        at = pl.ds(b * MAPX, MAPX)
+        return pltpu.make_async_copy(moved_ref.at[at, :], moved_out.at[at, :], out_sem.at[b])
+
     n_stage = len(bits)
     rs_copy(0).start()
+    forward(half - 2)
     row_coefs()
     for b in range(1, rb - 1):
         row_block(V, H, to_y, b)
@@ -319,13 +396,13 @@
     def halo_wait(d):
         @pl.when(has_up)
         def _():
-            hcopy(d, 0).wait_send()
             hcopy(d, 1).wait_recv()
 
         @pl.when(has_down)
         def _():
-            hcopy(d, 1).wait_send()
             hcopy(d, 0).wait_recv()
+        for lower in (0, 1):
+            hsent(d, lower)
 
     for s in reversed(range(n_stage)):
         ag_copy(s).start()
@@ -336,14 +413,21 @@
             row_block(V, H, to_y, rb - 1)
             for b in range(1, rb - 1):
                 row_block(Y, MAPX, to_out, b)
+                put(b).start()
         ag_copy(s).wait()
-    obs_out[...] = obs[...]
+    obs_put = pltpu.make_async_copy(obs, obs_out, out_sem.at[rb])
+    obs_put.start()
     for d in range(half // 2, half):
         halo_wait(d)
     row_block(V, H, to_y, -1)
     row_block(V, H, to_y, rb)
     row_block(Y, MAPX, to_out, 0)
+    put(0).start()
     row_block(Y, MAPX, to_out, rb - 1)
+    put(rb - 1).start()
+    obs_put.wait()
+    for b in range(rb):
+        put(b).wait()
 
 
 def observe_block(V, ah, al, part, b, first, H, cols):
@@ -375,14 +459,22 @@
     nchunk = rows // CHUNK
     stages = nr.bit_length() - 1
     f32, bf16 = jnp.float32, jnp.bfloat16
-    vmem = pl.BlockSpec(memory_space=pltpu.VMEM)
     dma = pltpu.SemaphoreType.DMA
     moved, obs = pl.pallas_call(
         functools.partial(kernel, nr, nc),
         out_shape=(jax.ShapeDtypeStruct((rows, cols), f32), jax.ShapeDtypeStruct((n_obs, cols), f32)),
-        in_specs=[pl.BlockSpec(memory_space=pl.ANY), vmem, vmem, vmem, pl.BlockSpec(memory_space=pltpu.SMEM)],
-        out_specs=(vmem, vmem),
+        in_specs=[pl.BlockSpec(memory_space=pltpu.HBM)] * 5,
+        out_specs=(pl.BlockSpec(memory_space=pltpu.HBM),) * 2,
         scratch_shapes=[
+            pltpu.VMEM((rows, cols), f32),
+            dma((rb + 1,)),
+            pltpu.VMEM(wind_mask.shape, jnp.int32),
+            pltpu.VMEM(wind_speed.shape, f32),
+            pltpu.VMEM(obs_cells.shape, jnp.int32),
+            pltpu.SMEM(obs_scale.shape, f32),
+            dma((4,)),
+            pltpu.VMEM((nchunk // 4, nl, CHUNK, LANES), f32),
+            dma((nchunk // 4,)), dma((nchunk // 4,)), dma((nchunk // 4,)),
             pltpu.VMEM((rows, cols), f32),
             pltpu.VMEM((rows, cols), f32),
             pltpu.VMEM((rows, cols), f32),
@@ -405,7 +497,7 @@
             dma((stages,)), dma((stages,)), dma((stages,)), dma((stages,)),
         ],
         compiler_params=pltpu.CompilerParams(
-            collective_id=0, has_side_effects=True, vmem_limit_bytes=48 * 1024 * 1024),
+            collective_id=0, has_side_effects=True, vmem_limit_bytes=60 * 1024 * 1024),
         cost_estimate=pl.CostEstimate(flops=2 * 10 ** 9, bytes_accessed=10 ** 7, transcendentals=0),
     )(covariance, wind_mask, wind_speed, obs_cells, obs_scale)
     block = MAPX
@@ -420,7 +512,7 @@
         ],
         out_specs=pl.BlockSpec((block, cols), lambda i: (i, 0)),
         cost_estimate=pl.CostEstimate(flops=10 ** 9, bytes_accessed=5 * 10 ** 6, transcendentals=0),
-        compiler_params=pltpu.CompilerParams(vmem_limit_bytes=24 * 1024 * 1024),
+        compiler_params=pltpu.CompilerParams(vmem_limit_bytes=60 * 1024 * 1024),
     )(moved, gain, obs)
 
 

time: 79.8 us -> 69.8 us (0.87)
  Pallas kernels: 74.7 us -> 69.1 us
  local copies, waits for them, and re-layouts: 4.75 us -> 0 us
    pallas_call x1, Pallas kernels: 72.1 us -> 64.3 us  [local(): pl.pallas_call(functools.partial(kernel, nr, nc), out_shape=(jax.ShapeDty...]
    unnamed x12 -> x0, local copies, waits for them, and re-layouts: 4.75 us -> none
    pallas_call x1, Pallas kernels: 2.6 us -> 4.76 us  [local(): pl.pallas_call(update_kernel, grid=(rows // block,), out_shape=jax.ShapeD...]
where the time goes in v2:
time: 69.8 us; the launch traced here: 69.1 us
  Pallas kernels  69.1 us (99%)
    pallas_call x1, Pallas kernels, local(): pl.pallas_call(functools.partial(kernel, nr, nc), out_shape=(jax.ShapeDty...  64.3 us
    pallas_call x1, Pallas kernels, local(): pl.pallas_call(update_kernel, grid=(rows // block,), out_shape=jax.ShapeD...  4.76 us

profile of v2, /device:TPU:8, one launch (start us, length us, event | category | flops | bytes accessed | tf_op | source)
XLA Modules:
  0.0 69.1 jit_solution(12910058415896134060)
XLA Ops:
  0.0 64.3 %shard_map.64 = (f32[1024,512]{1,0:T(8,128)}, f32[256,512]{1,0:T(8,128)}) custom-call(f32[1024,512]{1,0:T(8,128)} %cov.1, s32[2,4096]{1,0:T(2,128)} %mask_hbm.1, f32[2,4096]{1,0:T(2,128)} %speed_hbm.1, s32[256,128]{1,0:T(8,128)} %cells_hbm.1, f32[256]{0:T(256)} %scale_hbm.1), custom_call_target="tpu_custom_call" | custom-call | flops 2000000000 | bytes 10000000 | tf_op jit(solution)/shard_map/pallas_call | solution.py:463
  64.3 4.8 %shard_map.65 = f32[1024,512]{1,0:T(8,128)} custom-call(f32[1024,512]{1,0:T(8,128)} %get-tuple-element.7.moved_ref, bf16[1024,256]{1,0:T(8,128)(2,1)} %gain_ref.1, f32[256,512]{1,0:T(8,128)} %get-tuple-element.8.obs_ref), custom_call_target="tpu_custom_call" | custom-call | flops 1000000000 | bytes 5000000 | tf_op jit(solution)/shard_map/pallas_call | solution.py:504

commit v3 on v2

--- a/solution.py
+++ b/solution.py
@@ -46,9 +46,9 @@
 
 
 def kernel(
-    nr, nc, cov, mask_hbm, speed_hbm, cells_hbm, scale_hbm,
-    moved_out, obs_out,
-    moved_ref, out_sem,
+    nr, nc, cov, mask_hbm, speed_hbm, cells_hbm, scale_hbm, gain_hbm,
+    moved_out,
+    gain_ref, moved_ref, out_sem,
     mask_ref, speed_ref, cells_ref, scale_ref, in_sem, relay_buf, rl_s, rl_r, fw_s,
     own, lh, rh, V, Y, ccol, crow, rc, sbuf, s2, tbuf, ah, al, part, rsbuf, obs,
     own_sem, zs, zr, hs, hr, rs_s, rs_r, ag_s, ag_r,
@@ -86,7 +86,8 @@
     small = [
         pltpu.make_async_copy(src, dst, in_sem.at[i])
         for i, (src, dst) in enumerate((
-            (mask_hbm, mask_ref), (speed_hbm, speed_ref), (cells_hbm, cells_ref), (scale_hbm, scale_ref)))
+            (mask_hbm, mask_ref), (speed_hbm, speed_ref), (cells_hbm, cells_ref), (scale_hbm, scale_ref),
+            (gain_hbm, gain_ref)))
     ]
     for copy in small:
         copy.start()
@@ -184,8 +185,8 @@
         def _():
             hcopy(d, lower).wait_send()
 
-    def zstart(d, _):
-        for lower in (0, 1):
+    def zstart(d, lowers=(0, 1)):
+        for lower in lowers:
             @pl.when(has_left)
             def _():
                 zcopy(d, lower, 0).start()
@@ -193,9 +194,8 @@
             @pl.when(has_right)
             def _():
                 zcopy(d, lower, 1).start()
-        return 0
-
-    lax.fori_loop(0, half, zstart, 0)
+
+    zstart(0)
 
     @pl.when(jnp.logical_not(has_left))
     def _():
@@ -274,11 +274,19 @@
             @pl.when(has_left)
             def _():
                 zcopy(d, lower, 0).wait_send()
+
+            @pl.when(has_right)
+            def _():
+                zcopy(d, lower, 1).wait_send()
+            if d + 1 < half:
+                zstart(d + 1, (lower,))
+
+            @pl.when(has_left)
+            def _():
                 zcopy(d, lower, 1).wait_recv()
 
             @pl.when(has_right)
             def _():
-                zcopy(d, lower, 1).wait_send()
                 zcopy(d, lower, 0).wait_recv()
             col_chunk(chunk_base(d, lower))
             hstart(d, lower)
@@ -376,6 +384,11 @@
     def to_out(l, r0, r):
         moved_ref[pl.ds(pl.multiple_of(r0, 8), TILE), l * LANES:(l + 1) * LANES] = r
 
+    def to_final(l, r0, r):
+        at = pl.ds(pl.multiple_of(r0, 8), TILE)
+        where = slice(l * LANES, (l + 1) * LANES)
+        moved_ref[at, where] = r - moved_ref[at, where]
+
     def put(b):
         at = pl.ds(b * MAPX, MAPX)
         return pltpu.make_async_copy(moved_ref.at[at, :], moved_out.at[at, :], out_sem.at[b])
@@ -413,19 +426,24 @@
             row_block(V, H, to_y, rb - 1)
             for b in range(1, rb - 1):
                 row_block(Y, MAPX, to_out, b)
-                put(b).start()
         ag_copy(s).wait()
-    obs_put = pltpu.make_async_copy(obs, obs_out, out_sem.at[rb])
-    obs_put.start()
+    o_hi, o_lo = split(obs[...])
+    for b in range(rb):
+        at = slice(b * MAPX, (b + 1) * MAPX)
+        update = dot(gain_ref[at, :], o_hi) + dot(gain_ref[at, :], o_lo)
+        if 0 < b < rb - 1:
+            moved_ref[at, :] = moved_ref[at, :] - update
+            put(b).start()
+        else:
+            moved_ref[at, :] = update
     for d in range(half // 2, half):
         halo_wait(d)
     row_block(V, H, to_y, -1)
     row_block(V, H, to_y, rb)
-    row_block(Y, MAPX, to_out, 0)
+    row_block(Y, MAPX, to_final, 0)
     put(0).start()
-    row_block(Y, MAPX, to_out, rb - 1)
+    row_block(Y, MAPX, to_final, rb - 1)
     put(rb - 1).start()
-    obs_put.wait()
     for b in range(rb):
         put(b).wait()
 
@@ -444,12 +462,6 @@
             part[:, at] = part[:, at] + r
 
 
-def update_kernel(moved_ref, gain_ref, obs_ref, out_ref):
-    o_hi, o_lo = split(obs_ref[...])
-    g = gain_ref[...]
-    out_ref[...] = moved_ref[...] - (dot(g, o_hi) + dot(g, o_lo))
-
-
 def local(nr, nc, covariance, wind_mask, wind_speed, obs_cells, obs_scale, gain):
     rows, cols = covariance.shape
     n_obs = obs_cells.shape[0]
@@ -460,19 +472,20 @@
     stages = nr.bit_length() - 1
     f32, bf16 = jnp.float32, jnp.bfloat16
     dma = pltpu.SemaphoreType.DMA
-    moved, obs = pl.pallas_call(
+    return pl.pallas_call(
         functools.partial(kernel, nr, nc),
-        out_shape=(jax.ShapeDtypeStruct((rows, cols), f32), jax.ShapeDtypeStruct((n_obs, cols), f32)),
-        in_specs=[pl.BlockSpec(memory_space=pltpu.HBM)] * 5,
-        out_specs=(pl.BlockSpec(memory_space=pltpu.HBM),) * 2,
+        out_shape=jax.ShapeDtypeStruct((rows, cols), f32),
+        in_specs=[pl.BlockSpec(memory_space=pltpu.HBM)] * 6,
+        out_specs=pl.BlockSpec(memory_space=pltpu.HBM),
         scratch_shapes=[
+            pltpu.VMEM(gain.shape, bf16),
             pltpu.VMEM((rows, cols), f32),
-            dma((rb + 1,)),
+            dma((rb,)),
             pltpu.VMEM(wind_mask.shape, jnp.int32),
             pltpu.VMEM(wind_speed.shape, f32),
             pltpu.VMEM(obs_cells.shape, jnp.int32),
             pltpu.SMEM(obs_scale.shape, f32),
-            dma((4,)),
+            dma((5,)),
             pltpu.VMEM((nchunk // 4, nl, CHUNK, LANES), f32),
             dma((nchunk // 4,)), dma((nchunk // 4,)), dma((nchunk // 4,)),
             pltpu.VMEM((rows, cols), f32),
@@ -499,21 +512,7 @@
         compiler_params=pltpu.CompilerParams(
             collective_id=0, has_side_effects=True, vmem_limit_bytes=60 * 1024 * 1024),
         cost_estimate=pl.CostEstimate(flops=2 * 10 ** 9, bytes_accessed=10 ** 7, transcendentals=0),
-    )(covariance, wind_mask, wind_speed, obs_cells, obs_scale)
-    block = MAPX
-    return pl.pallas_call(
-        update_kernel,
-        grid=(rows // block,),
-        out_shape=jax.ShapeDtypeStruct((rows, cols), f32),
-        in_specs=[
-            pl.BlockSpec((block, cols), lambda i: (i, 0)),
-            pl.BlockSpec((block, n_obs), lambda i: (i, 0)),
-            pl.BlockSpec((n_obs, cols), lambda i: (0, 0)),
-        ],
-        out_specs=pl.BlockSpec((block, cols), lambda i: (i, 0)),
-        cost_estimate=pl.CostEstimate(flops=10 ** 9, bytes_accessed=5 * 10 ** 6, transcendentals=0),
-        compiler_params=pltpu.CompilerParams(vmem_limit_bytes=60 * 1024 * 1024),
-    )(moved, gain, obs)
+    )(covariance, wind_mask, wind_speed, obs_cells, obs_scale, gain)
 
 
 def solution(mesh):

time: 69.8 us -> 69 us (0.989)
  Pallas kernels: 69.1 us -> 65.8 us
  local copies, waits for them, and re-layouts: 0 us -> 3.08 us
    pallas_call x2 -> x1, Pallas kernels: 69.1 us -> 65.8 us  [local(): pl.pallas_call(functools.partial(kernel, nr, nc), out_shape=jax.ShapeDtyp...]
    unnamed x0 -> x1, local copies, waits for them, and re-layouts: none -> 3.08 us
where the time goes in v3:
time: 69 us; the launch traced here: 68.9 us
  Pallas kernels  65.8 us (95%)
  local copies, waits for them, and re-layouts  3.08 us (4%)
    pallas_call x1, Pallas kernels, local(): pl.pallas_call(functools.partial(kernel, nr, nc), out_shape=jax.ShapeDtyp...  65.8 us
    unnamed x1, local copies, waits for them, and re-layouts  3.08 us

profile of v3, /device:TPU:8, one launch (start us, length us, event | category | flops | bytes accessed | tf_op | source)
XLA Modules:
  0.0 68.9 jit_solution(880645680022584775)
XLA Ops:
  0.0 65.8 %shard_map.64 = f32[1024,512]{1,0:T(8,128)} custom-call(f32[1024,512]{1,0:T(8,128)} %cov.1, s32[2,4096]{1,0:T(2,128)} %mask_hbm.1, f32[2,4096]{1,0:T(2,128)} %speed_hbm.1, s32[256,128]{1,0:T(8,128)} %cells_hbm.1, f32[256]{0:T(256)} %scale_hbm.1, bf16[1024,256]{1,0:T(8,128)(2,1)} %gain_hbm.1), custom_call_target="tpu_custom_call" | custom-call | flops 2000000000 | bytes 10000000 | tf_op jit(solution)/shard_map/pallas_call | solution.py:475
  65.8 3.1 %copy.8 = f32[1024,512]{1,0:T(8,128)} copy(f32[1024,512]{1,0:T(8,128)} %shard_map.64) | data formatting | bytes 4194304
